TPU v7x, 32 devices: a whole 2x2x4 slice. The times are simulated.
32 devices in a mesh: slab: 2 (over y), tile: 4 (over z), gz: 2 (over x), ang: 2 (over core).
Axes of the slice: x: 2, y: 2, z: 4, core: 2. Of those that a mesh axis runs over, the one named last changes fastest.
Arguments:
- primal: float32 [32, 8192], P(('slab', 'gz'), 'tile'), parts along dimension 0, may hold values from -6 to 6
- dual: float32 [32, 64, 2048], P(('slab', 'gz'), ('ang', 'tile')), parts along dimension 0, may hold values from -6 to 6
- data: float32 [32, 64, 2048], P(('slab', 'gz'), ('ang', 'tile')), parts along dimension 0, may hold values from -6 to 6
- blocks: bfloat16 [4, 64, 2048, 128], P('tile', 'ang'), may hold values from -0.125 to 0.125
- offsets: int32 [4, 64], P(None, 'ang'), may hold values from 0 to 1920
- incidence: int32 [4, 64], P(None, 'ang'), may hold values 0 or 1
- dual_in: float32 [3, 32], replicated, may hold values from -4 to 4
- dual_bias: float32 [32], replicated, may hold values from -3 to 3
- dual_out: float32 [32], replicated, may hold values from -1 to 1
- kernel_in: float32 [3, 2, 32], replicated, may hold values from -2.5 to 2.5
- kernel_bias: float32 [32], replicated, may hold values from -3 to 3
- kernel_out: float32 [3, 32], replicated, may hold values from -0.625 to 0.625
- cot_primal: float32 [32, 8192], P(('slab', 'gz'), 'tile'), parts along dimension 0, may hold values from -6 to 6
- cot_dual: float32 [32, 64, 2048], P(('slab', 'gz'), ('ang', 'tile')), parts along dimension 0, may hold values from -6 to 6
Outputs:
- grad_primal: float32 [32, 8192], P(('slab', 'gz'), 'tile'), parts along dimension 0
- grad_dual: float32 [32, 64, 2048], P(('slab', 'gz'), ('ang', 'tile')), parts along dimension 0
- grad_data: float32 [32, 64, 2048], P(('slab', 'gz'), ('ang', 'tile')), parts along dimension 0
There are 2 independent parts, one for each index of `slab`. A program takes and returns all parts, laid end to end along the dimension named above; an argument that names none is the same for every part. Nothing has to cross between parts.
All inputs are finite; a program needn't handle non-finite values. No bound on the sum of `incidence` on one device may be relied on, other than what follows from the above.
Results may differ from a plain program's by a relative error of at most 0.0062.
Values may be sent and summed in bfloat16 or wider, within the bound.
A program may use at most 128 MiB of HBM per device.

v0:
```python
import functools

import jax
import jax.numpy as jnp
from jax import lax
from jax.experimental import pallas as pl
from jax.experimental.pallas import tpu as pltpu
from jax.sharding import PartitionSpec as P

LANES = 128
K1 = 0.7978845608028654
K3 = K1 * 0.044715
F32 = jnp.float32
BF16 = jnp.bfloat16
MESH = pl.DeviceIdType.MESH


def kernel(
    tiles, groups, cores,
    primal, dual, data, blocks, offsets, incidence, dual_in, dual_bias, dual_out,
    kernel_in, kernel_bias, kernel_out, cot_primal, cot_dual,
    grad_primal, grad_dual, grad_data,
    held, psend, precv, dstage, dsend, drecv, slopes, sino, fresh, turn, turn2, dense_primal,
    dense_cot, dense_back, hsend, hpart, hedge, gsend, gpart,
    load_sem, psend_sem, precv_sem, dsend_sem, drecv_sem, edge_send, edge_recv,
    hsend_sem, hrecv_sem, hedge_send, hedge_recv, gsend_sem, grecv_sem,
):
    rows = primal.shape[0]
    own = dual.shape[1]
    nb = dual.shape[2] // LANES
    np_ = primal.shape[1] // LANES
    chans = dual_bias.shape[0]
    me = lax.axis_index("tile")
    gz = lax.axis_index("gz")
    ang = lax.axis_index("ang")

    def owner_at(i):
        return lax.rem(me + i, tiles)

    loads = []
    for i in range(tiles):
        o = owner_at(i + 1)
        copy = pltpu.make_async_copy(
            blocks.at[pl.ds(o * own, own)], held.at[pl.ds(o * own, own)], load_sem.at[i]
        )
        copy.start()
        loads.append(copy)

    barrier = pltpu.get_barrier_semaphore()
    for i in range(1, tiles):
        pl.semaphore_signal(barrier, inc=1, device_id={"tile": owner_at(i)}, device_id_type=MESH)
    for i in range(1, cores):
        pl.semaphore_signal(
            barrier, inc=1, device_id={"ang": lax.rem(ang + i, cores)}, device_id_type=MESH
        )
    for has, step in ((gz > 0, -1), (gz < groups - 1, 1)):
        @pl.when(has)
        def _():
            for core in range(cores):
                pl.semaphore_signal(
                    barrier, inc=1, device_id={"gz": gz + step, "ang": core}, device_id_type=MESH
                )
    sides = (gz > 0).astype(jnp.int32) + (gz < groups - 1).astype(jnp.int32)
    if groups == 2:
        sides = 1
    pl.semaphore_wait(barrier, tiles - 1 + cores - 1 + cores * sides)

    def to_dense(value, target, first):
        for b in range(np_):
            turn[b * rows : (b + 1) * rows, :] = value[:, b * LANES : (b + 1) * LANES]
        for z in range(rows):
            target[(first + z) * np_ : (first + z + 1) * np_, :] = turn[pl.ds(z, np_, stride=rows), :]

    to_dense(primal[...], dense_primal, 2)
    to_dense(cot_primal[...], dense_cot, 2)
    edge = 2 * np_
    low_in = pl.ds(0, edge)
    low_own = pl.ds(edge, edge)
    high_own = pl.ds(rows * np_, edge)
    high_in = pl.ds((rows + 2) * np_, edge)

    def edge_copies(step):
        src, dst, side = (low_own, high_in, 0) if step < 0 else (high_own, low_in, 1)
        return [
            pltpu.make_async_remote_copy(
                src_ref=ref.at[src], dst_ref=ref.at[dst],
                send_sem=edge_send.at[side, n], recv_sem=edge_recv.at[side, n],
                device_id={"gz": gz + step}, device_id_type=MESH,
            )
            for n, ref in enumerate((dense_primal, dense_cot))
        ]

    for has, step in ((gz > 0, -1), (gz < groups - 1, 1)):
        @pl.when(has)
        def _():
            for copy in edge_copies(step):
                copy.start()

        @pl.when(jnp.logical_not(has))
        def _():
            where = low_in if step < 0 else high_in
            for ref in (dense_primal, dense_cot, dense_back):
                ref[where, :] = jnp.zeros((edge, LANES), F32)

    lane = lax.broadcasted_iota(jnp.int32, (own, LANES), 1)
    sub = lax.broadcasted_iota(jnp.int32, (own, LANES), 0)

    def home_blocks():
        result = []
        for t in range(tiles):
            at = jnp.zeros((own, LANES), jnp.int32)
            for j in range(own):
                at = jnp.where(sub == j, offsets[t, me * own + j], at)
            result.append((at >> 7) + (lane < (at & (LANES - 1))).astype(jnp.int32))
        return result

    def pcopy(ph, i):
        return pltpu.make_async_remote_copy(
            src_ref=psend.at[ph, i], dst_ref=precv.at[ph, me],
            send_sem=psend_sem.at[ph, i], recv_sem=precv_sem.at[ph, me],
            device_id={"tile": owner_at(i)}, device_id_type=MESH,
        )

    def dcopy(ph, i):
        return pltpu.make_async_remote_copy(
            src_ref=dsend.at[ph, i], dst_ref=drecv.at[ph, me],
            send_sem=dsend_sem.at[ph, i], recv_sem=drecv_sem.at[ph, me],
            device_id={"tile": owner_at(i)}, device_id_type=MESH,
        )

    def await_recv(buffer, sem, ph, i):
        o = owner_at(i)
        pltpu.make_async_remote_copy(
            src_ref=buffer.at[ph, o], dst_ref=buffer.at[ph, o],
            send_sem=sem.at[ph, o], recv_sem=sem.at[ph, o],
            device_id={"tile": o}, device_id_type=MESH,
        ).wait_recv()

    def pair_of(a):
        return jnp.concatenate([held[a], held[a + 1]], axis=1)

    def project(image, ph):
        for i in list(range(1, tiles)) + [0]:
            o = owner_at(i)
            if ph == 0:
                loads[(i - 1) % tiles].wait()

            def step(j, carry):
                a = o * own + 2 * j
                both = jnp.dot(image, pair_of(a), preferred_element_type=F32)
                for h in range(2):
                    part = both[:, h * LANES : (h + 1) * LANES]
                    part = part * incidence[me, a + h].astype(F32)
                    part = pltpu.roll(part, offsets[me, a + h] & (LANES - 1), 1)
                    where = pl.ds((2 * j + h) * rows, rows)
                    if i == 0:
                        precv[ph, me, where, :] = part
                    else:
                        psend[ph, i, where, :] = part
                return carry

            lax.fori_loop(0, own // 2, step, 0)
            if i > 0:
                pcopy(ph, i).start()
        for i in range(1, tiles):
            await_recv(precv, precv_sem, ph, i)

    def place(ph, z, homes):
        windows = [precv.at[ph, t][pl.ds(z, own, stride=rows), :] for t in range(tiles)]
        result = []
        for b in range(nb):
            total = jnp.zeros((own, LANES), F32)
            for t in range(tiles):
                total = total + jnp.where(homes[t] == b, windows[t], 0.0)
            result.append(total)
        return result

    def take(values, z, homes):
        for t in range(tiles):
            total = jnp.zeros((own, LANES), F32)
            for b in range(nb):
                total = jnp.where(homes[t] == b, values[b], total)
            dstage.at[t][pl.ds(z, own, stride=rows), :] = total

    def send_windows(ph):
        for i in range(1, tiles):
            dsend[ph, i] = dstage[owner_at(i)].astype(BF16)
            dcopy(ph, i).start()
        drecv[ph, me] = dstage[me].astype(BF16)

    def back(ph):
        total = jnp.zeros((rows, np_ * LANES), F32)
        for i in range(tiles):
            o = owner_at(i)
            if i > 0:
                await_recv(drecv, drecv_sem, ph, i)

            def step(j, total):
                a = o * own + 2 * j
                both = drecv[ph, o, pl.ds(pl.multiple_of(2 * rows * j, 2 * rows), 2 * rows), :].astype(F32)
                parts = []
                for h in range(2):
                    part = both[h * rows : (h + 1) * rows] * incidence[me, a + h].astype(F32)
                    shift = (LANES - (offsets[me, a + h] & (LANES - 1))) & (LANES - 1)
                    parts.append(pltpu.roll(part, shift, 1))
                both = jnp.concatenate(parts, axis=1).astype(BF16)
                return total + lax.dot_general(
                    both, pair_of(a), (((1,), (1,)), ((), ())), preferred_element_type=F32
                )

            total = lax.fori_loop(0, own // 2, step, total)
        return total

    project(primal[...].astype(BF16), 0)
    group = 4
    unroll = 8

    def dual_row(z, carry):
        homes = home_blocks()
        for b, value in enumerate(place(0, z, homes)):
            sino[:, b * LANES : (b + 1) * LANES] = value

        def dual_piece(g, carry):
            cols = [
                pl.ds(pl.multiple_of((g * group + n) * LANES, LANES), LANES) for n in range(group)
            ]
            ds = [dual[z, :, col] for col in cols]
            ss = [sino[:, col] for col in cols]
            xs = [data[z, :, col] for col in cols]

            def channels(cu, sums):
                sums = [list(s) for s in sums]
                for k in range(unroll):
                    c = cu * unroll + k
                    w0, w1, w2 = dual_in[0, c], dual_in[1, c], dual_in[2, c]
                    bias, half = dual_bias[c], 0.5 * dual_out[c]
                    h0, h1, h2 = half * w0, half * w1, half * w2
                    for n in range(group):
                        x = w0 * ds[n] + w1 * ss[n] + w2 * xs[n] + bias
                        x2 = x * x
                        t = jnp.tanh(x * (K1 + K3 * x2))
                        up = 1.0 + t
                        slope = up * (1.0 + x * (1.0 - t) * (K1 + 3.0 * K3 * x2))
                        sums[0][n] = sums[0][n] + half * (x * up)
                        sums[1][n] = sums[1][n] + h0 * slope
                        sums[2][n] = sums[2][n] + h1 * slope
                        sums[3][n] = sums[3][n] + h2 * slope
                return tuple(tuple(s) for s in sums)

            zero = tuple(jnp.zeros((own, LANES), F32) for _ in range(group))
            sums = lax.fori_loop(0, chans // unroll, channels, (zero,) * 4)
            for n, col in enumerate(cols):
                fresh[:, col] = ds[n] + sums[0][n]
                for k in range(3):
                    slopes[k, z, :, col] = sums[k + 1][n]
            return carry

        lax.fori_loop(0, nb // group, dual_piece, 0)
        take([fresh[:, b * LANES : (b + 1) * LANES] for b in range(nb)], z, homes)
        return carry

    lax.fori_loop(0, rows, dual_row, 0)
    send_windows(0)

    to_dense(back(0), hsend, 0)

    def hcopy(i):
        return pltpu.make_async_remote_copy(
            src_ref=hsend, dst_ref=hpart.at[ang],
            send_sem=hsend_sem.at[i], recv_sem=hrecv_sem.at[ang],
            device_id={"ang": lax.rem(ang + i, cores)}, device_id_type=MESH,
        )

    def hedge_copies(step):
        src, side = (pl.ds(0, edge), 1) if step < 0 else (pl.ds((rows - 2) * np_, edge), 0)
        return [
            pltpu.make_async_remote_copy(
                src_ref=hsend.at[src], dst_ref=hedge.at[side, ang],
                send_sem=hedge_send.at[side, core], recv_sem=hedge_recv.at[side, ang],
                device_id={"gz": gz + step, "ang": core}, device_id_type=MESH,
            )
            for core in range(cores)
        ]

    for has, step in ((gz > 0, -1), (gz < groups - 1, 1)):
        @pl.when(has)
        def _():
            for copy in hedge_copies(step):
                copy.start()
    for i in range(1, cores):
        hcopy(i).start()
    hpart[ang] = hsend[...]

    for has, step in ((gz > 0, -1), (gz < groups - 1, 1)):
        @pl.when(has)
        def _():
            side = 1 if step < 0 else 0
            for copy in edge_copies(-step):
                copy.wait_recv()
            total = jnp.zeros((edge, LANES), F32)
            for core in range(cores):
                pltpu.make_async_remote_copy(
                    src_ref=hedge.at[1 - side, core], dst_ref=hedge.at[1 - side, core],
                    send_sem=hedge_recv.at[1 - side, core], recv_sem=hedge_recv.at[1 - side, core],
                    device_id={"gz": gz + step, "ang": core}, device_id_type=MESH,
                ).wait_recv()
                total = total + hedge[1 - side, core]
            dense_back[low_in if step < 0 else high_in, :] = total
    for i in range(1, cores):
        other = lax.rem(ang + i, cores)
        pltpu.make_async_remote_copy(
            src_ref=hpart.at[other], dst_ref=hpart.at[other],
            send_sem=hrecv_sem.at[other], recv_sem=hrecv_sem.at[other],
            device_id={"ang": other}, device_id_type=MESH,
        ).wait_recv()
    total = hpart[0]
    for core in range(1, cores):
        total = total + hpart[core]
    dense_back[pl.ds(edge, rows * np_), :] = total

    keep_low = (gz > 0).astype(F32)
    keep_high = (gz < groups - 1).astype(F32)

    def pixel_piece(h, carry):
        def at(ref, z):
            return ref[pl.ds(pl.multiple_of((z + 2) * np_ + h * 8, 8), 8), :]

        def channel(c, sums):
            sums = [list(s) for s in sums]
            kin = [[kernel_in[k, i, c] for i in range(2)] for k in range(3)]
            kout = [0.5 * kernel_out[k, c] for k in range(3)]
            bias = kernel_bias[c]
            for z in range(-1, rows + 1):
                x = bias + jnp.zeros((8, LANES), F32)
                hid = None
                for k in range(3):
                    x = x + kin[k][0] * at(dense_primal, z + k - 1)
                    x = x + kin[k][1] * at(dense_back, z + k - 1)
                    term = kout[k] * at(dense_cot, z - k + 1)
                    hid = term if hid is None else hid + term
                x2 = x * x
                t = jnp.tanh(x * (K1 + K3 * x2))
                grad = hid * ((1.0 + t) * (1.0 + x * (1.0 - t) * (K1 + 3.0 * K3 * x2)))
                if z < 0:
                    grad = grad * keep_low
                if z == rows:
                    grad = grad * keep_high
                for k in range(3):
                    out = z + k - 1
                    if 0 <= out < rows:
                        for i in range(2):
                            sums[i][out] = sums[i][out] + kin[k][i] * grad
            return tuple(tuple(s) for s in sums)

        zero = tuple(jnp.zeros((8, LANES), F32) for _ in range(rows))
        sums = lax.fori_loop(0, chans, channel, (zero,) * 2)
        for z in range(rows):
            turn[pl.ds(h * 8 * rows + z, 8, stride=rows), :] = sums[1][z]
            turn2[pl.ds(h * 8 * rows + z, 8, stride=rows), :] = sums[0][z]
        return carry

    lax.fori_loop(0, np_ // 8, pixel_piece, 0)
    image = jnp.concatenate([turn[b * rows : (b + 1) * rows, :] for b in range(np_)], axis=1)

    project(image.astype(BF16), 1)

    def grad_row(z, carry):
        homes = home_blocks()
        outs = []
        for b, value in enumerate(place(1, z, homes)):
            col = slice(b * LANES, (b + 1) * LANES)
            value = value + cot_dual[z, :, col]
            grad_dual[z, :, col] = value + value * slopes[0, z, :, col]
            grad_data[z, :, col] = value * slopes[2, z, :, col]
            outs.append(value * slopes[1, z, :, col])
        take(outs, z, homes)
        return carry

    lax.fori_loop(0, rows, grad_row, 0)
    send_windows(1)
    gsend[...] = back(1)

    def gcopy(i):
        return pltpu.make_async_remote_copy(
            src_ref=gsend, dst_ref=gpart.at[ang],
            send_sem=gsend_sem.at[i], recv_sem=grecv_sem.at[ang],
            device_id={"ang": lax.rem(ang + i, cores)}, device_id_type=MESH,
        )

    for i in range(1, cores):
        gcopy(i).start()
    gpart[ang] = gsend[...]
    for i in range(1, cores):
        other = lax.rem(ang + i, cores)
        pltpu.make_async_remote_copy(
            src_ref=gpart.at[other], dst_ref=gpart.at[other],
            send_sem=grecv_sem.at[other], recv_sem=grecv_sem.at[other],
            device_id={"ang": other}, device_id_type=MESH,
        ).wait_recv()
    total = gpart[0]
    for core in range(1, cores):
        total = total + gpart[core]
    for b in range(np_):
        col = slice(b * LANES, (b + 1) * LANES)
        grad_primal[:, col] = (
            cot_primal[:, col] + turn2[b * rows : (b + 1) * rows, :] + total[:, col]
        )

    for ph in range(2):
        for i in range(1, tiles):
            pcopy(ph, i).wait_send()
            dcopy(ph, i).wait_send()
    for i in range(1, cores):
        hcopy(i).wait_send()
        gcopy(i).wait_send()
    for has, step in ((gz > 0, -1), (gz < groups - 1, 1)):
        @pl.when(has)
        def _():
            for copy in edge_copies(step) + hedge_copies(step):
                copy.wait_send()


def solution(mesh):
    tiles, groups, cores = mesh.shape["tile"], mesh.shape["gz"], mesh.shape["ang"]

    def local(primal, dual, data, blocks, *rest):
        rows, pixels = primal.shape
        own, bins = dual.shape[1:]
        np_ = pixels // LANES
        dma = pltpu.SemaphoreType.DMA
        vmem = pl.BlockSpec(memory_space=pltpu.VMEM)
        smem = pl.BlockSpec(memory_space=pltpu.SMEM)
        window = (own * rows, LANES)
        scratch = [
            pltpu.VMEM(blocks.shape[1:], BF16),
            pltpu.VMEM((2, tiles) + window, F32),
            pltpu.VMEM((2, tiles) + window, F32),
            pltpu.VMEM((tiles,) + window, F32),
            pltpu.VMEM((2, tiles) + window, BF16),
            pltpu.VMEM((2, tiles) + window, BF16),
            pltpu.VMEM((3, rows, own, bins), F32),
            pltpu.VMEM((own, bins), F32),
            pltpu.VMEM((own, bins), F32),
            pltpu.VMEM((np_ * rows, LANES), F32),
            pltpu.VMEM((np_ * rows, LANES), F32),
            pltpu.VMEM(((rows + 4) * np_, LANES), F32),
            pltpu.VMEM(((rows + 4) * np_, LANES), F32),
            pltpu.VMEM(((rows + 4) * np_, LANES), F32),
            pltpu.VMEM((rows * np_, LANES), F32),
            pltpu.VMEM((cores, rows * np_, LANES), F32),
            pltpu.VMEM((2, cores, 2 * np_, LANES), F32),
            pltpu.VMEM((rows, pixels), F32),
            pltpu.VMEM((cores, rows, pixels), F32),
            dma((tiles,)),
            dma((2, tiles)), dma((2, tiles)), dma((2, tiles)), dma((2, tiles)),
            dma((2, 2)), dma((2, 2)),
            dma((cores,)), dma((cores,)), dma((2, cores)), dma((2, cores)),
            dma((cores,)), dma((cores,)),
        ]
        shape = jax.ShapeDtypeStruct
        return pl.pallas_call(
            functools.partial(kernel, tiles, groups, cores),
            out_shape=(
                shape((rows, pixels), F32),
                shape((rows, own, bins), F32),
                shape((rows, own, bins), F32),
            ),
            in_specs=[vmem, vmem, vmem, pl.BlockSpec(memory_space=pl.ANY)] + [smem] * 8 + [vmem] * 2,
            out_specs=(vmem, vmem, vmem),
            scratch_shapes=scratch,
            compiler_params=pltpu.CompilerParams(
                collective_id=0, has_side_effects=True, vmem_limit_bytes=48 * 2**20
            ),
        )(primal, dual, data, blocks[0], *rest)

    image = P(("slab", "gz"), "tile")
    sinogram = P(("slab", "gz"), ("ang", "tile"), None)
    angles = P(None, "ang")
    return jax.shard_map(
        local,
        mesh=mesh,
        in_specs=(
            image, sinogram, sinogram, P("tile", "ang", None, None), angles, angles,
            P(), P(), P(), P(), P(), P(), image, sinogram,
        ),
        out_specs=(image, sinogram, sinogram),
        check_vma=False,
    )
```

profile of v0, /device:TPU:0, one launch (start us, length us, event | category | flops | bytes accessed | tf_op | source)
XLA Modules:
  0.0 77.6 jit_solution(11812030427543838630)
XLA Ops:
  0.6 0.0 copy-start
  0.6 1.0 %copy-done = f32[8,8,2048]{2,1,0:T(8,128)S(1)} copy-done((f32[8,8,2048]{2,1,0:T(8,128)S(1)}, f32[8,8,2048]{2,1,0:T(8,128)}, u32[]{:S(2)}) %copy-start) | copy-done | bytes 524312
  1.7 0.0 copy-start.1
  1.7 1.0 %copy-done.1 = f32[8,8,2048]{2,1,0:T(8,128)S(1)} copy-done((f32[8,8,2048]{2,1,0:T(8,128)S(1)}, f32[8,8,2048]{2,1,0:T(8,128)}, u32[]{:S(2)}) %copy-start.1) | copy-done | bytes 524312
  2.7 0.0 copy-start.2
  2.7 1.0 %copy-done.2 = f32[8,8,2048]{2,1,0:T(8,128)S(1)} copy-done((f32[8,8,2048]{2,1,0:T(8,128)S(1)}, f32[8,8,2048]{2,1,0:T(8,128)}, u32[]{:S(2)}) %copy-start.2) | copy-done | bytes 524312
  3.8 0.0 copy-start.3
  3.8 0.8 %copy-done.3 = f32[8,2048]{1,0:T(8,128)S(1)} copy-done((f32[8,2048]{1,0:T(8,128)S(1)}, f32[8,2048]{1,0:T(8,128)}, u32[]{:S(2)}) %copy-start.3) | copy-done | bytes 65560
  4.6 0.0 copy-start.4
  4.6 0.8 %copy-done.4 = f32[8,2048]{1,0:T(8,128)S(1)} copy-done((f32[8,2048]{1,0:T(8,128)S(1)}, f32[8,2048]{1,0:T(8,128)}, u32[]{:S(2)}) %copy-start.4) | copy-done | bytes 65560
  5.4 0.0 copy-start.5
  5.4 0.7 copy-done.5
  6.1 0.0 copy-start.6
  6.1 0.7 copy-done.6
  6.8 0.0 copy-start.7
  6.8 0.7 copy-done.7
  7.5 0.0 copy-start.8
  7.5 0.7 copy-done.8
  8.2 0.0 copy-start.9
  8.2 0.7 copy-done.9
  8.9 0.0 copy-start.10
  8.9 0.7 copy-done.10
  9.5 0.0 copy-start.11
  9.5 0.7 copy-done.11
  10.2 0.0 copy-start.12
  10.2 0.7 copy-done.12
  10.8 64.6 %shard_map.157 = (f32[8,2048]{1,0:T(8,128)S(1)}, f32[8,8,2048]{2,1,0:T(8,128)S(1)}, f32[8,8,2048]{2,1,0:T(8,128)S(1)}) custom-call(f32[8,2048]{1,0:T(8,128)S(1)} %copy-done.3, f32[8,8,2048]{2,1,0:T(8,128)S(1)} %copy-done, f32[8,8,2048]{2,1,0:T(8,128)S(1)} %copy-done.1, bf16[32,2048,128]{2,1,0:T(8,128)(2,1)} %bitcast.1, s32[4,32]{1,0:T(4,128)S(1)} %copy-done.6, ...), custom_call_target="tpu_custom_call" | custom-call | tf_op jit(solution)/shard_map/pallas_call | solution.py:461
  75.4 0.6 copy.20
  76.0 0.8 %copy.21 = f32[8,8,2048]{2,1,0:T(8,128)} copy(f32[8,8,2048]{2,1,0:T(8,128)S(1)} %get-tuple-element.7) | data formatting | bytes 1048576
  76.8 0.8 %copy.22 = f32[8,8,2048]{2,1,0:T(8,128)} copy(f32[8,8,2048]{2,1,0:T(8,128)S(1)} %get-tuple-element.8) | data formatting | bytes 1048576
Async XLA Ops:
  0.6 1.0 %copy-start = (f32[8,8,2048]{2,1,0:T(8,128)S(1)}, f32[8,8,2048]{2,1,0:T(8,128)}, u32[]{:S(2)}) copy-start(f32[8,8,2048]{2,1,0:T(8,128)} %dual.1) | copy-start | bytes 1572868
  1.7 1.0 %copy-start.1 = (f32[8,8,2048]{2,1,0:T(8,128)S(1)}, f32[8,8,2048]{2,1,0:T(8,128)}, u32[]{:S(2)}) copy-start(f32[8,8,2048]{2,1,0:T(8,128)} %data.1) | copy-start | bytes 1572868
  2.7 1.0 %copy-start.2 = (f32[8,8,2048]{2,1,0:T(8,128)S(1)}, f32[8,8,2048]{2,1,0:T(8,128)}, u32[]{:S(2)}) copy-start(f32[8,8,2048]{2,1,0:T(8,128)} %cot_dual.1) | copy-start | bytes 1572868
  3.8 0.8 %copy-start.3 = (f32[8,2048]{1,0:T(8,128)S(1)}, f32[8,2048]{1,0:T(8,128)}, u32[]{:S(2)}) copy-start(f32[8,2048]{1,0:T(8,128)} %primal.1) | copy-start | bytes 196612
  4.6 0.8 %copy-start.4 = (f32[8,2048]{1,0:T(8,128)S(1)}, f32[8,2048]{1,0:T(8,128)}, u32[]{:S(2)}) copy-start(f32[8,2048]{1,0:T(8,128)} %cot_primal.1) | copy-start | bytes 196612
  5.4 0.7 copy-start.5
  6.1 0.7 copy-start.6
  6.8 0.7 copy-start.7
  7.5 0.7 copy-start.8
  8.2 0.7 copy-start.9
  8.9 0.7 copy-start.10
  9.5 0.7 copy-start.11
  10.2 0.7 copy-start.12
where the time goes:
time: 78.1 us; the launch traced here: 77.6 us
  Pallas kernels  64.6 us (83%)
  local copies, waits for them, and re-layouts  12.4 us (16%)
    pallas_call x1, Pallas kernels, local(): pl.pallas_call(functools.partial(kernel, tiles, groups, cores), out_shape...  64.6 us
    unnamed x29, local copies, waits for them, and re-layouts  12.4 us

commit v1 on v0

--- a/solution.py
+++ b/solution.py
@@ -10,6 +10,8 @@
 LANES = 128
 K1 = 0.7978845608028654
 K3 = K1 * 0.044715
+SCALE = K3 ** (1.0 / 3.0)
+KY = K1 / SCALE
 F32 = jnp.float32
 BF16 = jnp.bfloat16
 MESH = pl.DeviceIdType.MESH
@@ -17,9 +19,12 @@
 
 def kernel(
     tiles, groups, cores,
-    primal, dual, data, blocks, offsets, incidence, dual_in, dual_bias, dual_out,
-    kernel_in, kernel_bias, kernel_out, cot_primal, cot_dual,
+    primal_hbm, dual_hbm, data_hbm, blocks, offsets_hbm, incidence_hbm, dual_in_hbm, dual_bias_hbm,
+    dual_out_hbm, kernel_in_hbm, kernel_bias_hbm, kernel_out_hbm, cot_primal_hbm, cot_dual_hbm,
     grad_primal, grad_dual, grad_data,
+    primal, dual, data, offsets, incidence, dual_in, dual_bias,
+    dual_out, kernel_in, kernel_bias, kernel_out, cot_primal, cot_dual, small_sem,
+    base, pixel_base, pixel_hid, pstage,
     held, psend, precv, dstage, dsend, drecv, slopes, sino, fresh, turn, turn2, dense_primal,
     dense_cot, dense_back, hsend, hpart, hedge, gsend, gpart,
     load_sem, psend_sem, precv_sem, dsend_sem, drecv_sem, edge_send, edge_recv,
@@ -37,6 +42,16 @@
     def owner_at(i):
         return lax.rem(me + i, tiles)
 
+    small = []
+    for n, (src, dst) in enumerate((
+        (dual_in_hbm, dual_in), (dual_bias_hbm, dual_bias), (dual_hbm, dual), (data_hbm, data),
+        (primal_hbm, primal), (cot_primal_hbm, cot_primal), (offsets_hbm, offsets),
+        (incidence_hbm, incidence), (dual_out_hbm, dual_out), (kernel_in_hbm, kernel_in),
+        (kernel_bias_hbm, kernel_bias), (kernel_out_hbm, kernel_out), (cot_dual_hbm, cot_dual),
+    )):
+        copy = pltpu.make_async_copy(src, dst, small_sem.at[n])
+        copy.start()
+        small.append(copy)
     loads = []
     for i in range(tiles):
         o = owner_at(i + 1)
@@ -71,6 +86,8 @@
         for z in range(rows):
             target[(first + z) * np_ : (first + z + 1) * np_, :] = turn[pl.ds(z, np_, stride=rows), :]
 
+    for copy in small:
+        copy.wait()
     to_dense(primal[...], dense_primal, 2)
     to_dense(cot_primal[...], dense_cot, 2)
     edge = 2 * np_
@@ -107,10 +124,10 @@
 
     def home_blocks():
         result = []
-        for t in range(tiles):
+        for i in range(tiles):
             at = jnp.zeros((own, LANES), jnp.int32)
             for j in range(own):
-                at = jnp.where(sub == j, offsets[t, me * own + j], at)
+                at = jnp.where(sub == j, offsets[owner_at(i), me * own + j], at)
             result.append((at >> 7) + (lane < (at & (LANES - 1))).astype(jnp.int32))
         return result
 
@@ -153,20 +170,21 @@
                     part = part * incidence[me, a + h].astype(F32)
                     part = pltpu.roll(part, offsets[me, a + h] & (LANES - 1), 1)
                     where = pl.ds((2 * j + h) * rows, rows)
-                    if i == 0:
-                        precv[ph, me, where, :] = part
-                    else:
-                        psend[ph, i, where, :] = part
+                    pstage[i, where, :] = part
                 return carry
 
             lax.fori_loop(0, own // 2, step, 0)
             if i > 0:
+                psend[ph, i] = pstage[i].astype(BF16)
                 pcopy(ph, i).start()
+
+    def projected(ph):
         for i in range(1, tiles):
             await_recv(precv, precv_sem, ph, i)
-
-    def place(ph, z, homes):
-        windows = [precv.at[ph, t][pl.ds(z, own, stride=rows), :] for t in range(tiles)]
+            pstage[i] = precv[ph, owner_at(i)].astype(F32)
+
+    def place(z):
+        windows = [pstage.at[i][pl.ds(z, own, stride=rows), :] for i in range(tiles)]
         result = []
         for b in range(nb):
             total = jnp.zeros((own, LANES), F32)
@@ -175,7 +193,7 @@
             result.append(total)
         return result
 
-    def take(values, z, homes):
+    def take(values, z):
         for t in range(tiles):
             total = jnp.zeros((own, LANES), F32)
             for b in range(nb):
@@ -184,9 +202,9 @@
 
     def send_windows(ph):
         for i in range(1, tiles):
-            dsend[ph, i] = dstage[owner_at(i)].astype(BF16)
+            dsend[ph, i] = dstage[i].astype(BF16)
             dcopy(ph, i).start()
-        drecv[ph, me] = dstage[me].astype(BF16)
+        drecv[ph, me] = dstage[0].astype(BF16)
 
     def back(ph):
         total = jnp.zeros((rows, np_ * LANES), F32)
@@ -211,55 +229,96 @@
             total = lax.fori_loop(0, own // 2, step, total)
         return total
 
+    homes = home_blocks()
+
+    def base_piece(at, carry):
+        zz, b = at // nb, at % nb
+        col = pl.ds(pl.multiple_of(b * LANES, LANES), LANES)
+        d = jnp.concatenate([dual[2 * zz, :, col], dual[2 * zz + 1, :, col]], axis=0)
+        x = jnp.concatenate([data[2 * zz, :, col], data[2 * zz + 1, :, col]], axis=0)
+        for c in range(chans):
+            base[zz, b, c] = (
+                (SCALE * dual_in[0, c]) * d + (SCALE * dual_in[2, c]) * x + SCALE * dual_bias[c]
+            )
+        return carry
+
+    lax.fori_loop(0, rows // 2 * nb, base_piece, 0)
+
     project(primal[...].astype(BF16), 0)
-    group = 4
+    for has, step in ((gz > 0, -1), (gz < groups - 1, 1)):
+        @pl.when(has)
+        def _():
+            for copy in edge_copies(-step):
+                copy.wait_recv()
+
+    def dense_at(ref, z, h):
+        return ref[pl.ds(pl.multiple_of((z + 2) * np_ + h * 8, 8), 8), :]
+
+    def pixel_first(at, carry):
+        h, c = at // chans, at % chans
+        for z in range(-1, rows + 1):
+            x = jnp.full((8, LANES), SCALE * kernel_bias[c], F32)
+            hid = jnp.zeros((8, LANES), F32)
+            for k in range(3):
+                x = x + (SCALE * kernel_in[k, 0, c]) * dense_at(dense_primal, z + k - 1, h)
+                hid = hid + (1.5 * kernel_out[k, c]) * dense_at(dense_cot, z - k + 1, h)
+            pixel_base[h, c, z + 1] = x
+            pixel_hid[h, c, z + 1] = hid
+        return carry
+
+    lax.fori_loop(0, np_ // 8 * chans, pixel_first, 0)
+    projected(0)
+    group = 2
     unroll = 8
 
-    def dual_row(z, carry):
-        homes = home_blocks()
-        for b, value in enumerate(place(0, z, homes)):
-            sino[:, b * LANES : (b + 1) * LANES] = value
+    def dual_row(zz, carry):
+        for n in range(2):
+            for b, value in enumerate(place(2 * zz + n)):
+                sino[n * own : (n + 1) * own, b * LANES : (b + 1) * LANES] = value
 
         def dual_piece(g, carry):
             cols = [
                 pl.ds(pl.multiple_of((g * group + n) * LANES, LANES), LANES) for n in range(group)
             ]
-            ds = [dual[z, :, col] for col in cols]
             ss = [sino[:, col] for col in cols]
-            xs = [data[z, :, col] for col in cols]
 
             def channels(cu, sums):
                 sums = [list(s) for s in sums]
                 for k in range(unroll):
                     c = cu * unroll + k
-                    w0, w1, w2 = dual_in[0, c], dual_in[1, c], dual_in[2, c]
-                    bias, half = dual_bias[c], 0.5 * dual_out[c]
-                    h0, h1, h2 = half * w0, half * w1, half * w2
+                    w1 = SCALE * dual_in[1, c]
+                    out = dual_out[c]
+                    half = (0.5 / SCALE) * out
+                    h0, h1, h2 = [1.5 * out * dual_in[m, c] for m in range(3)]
                     for n in range(group):
-                        x = w0 * ds[n] + w1 * ss[n] + w2 * xs[n] + bias
-                        x2 = x * x
-                        t = jnp.tanh(x * (K1 + K3 * x2))
+                        y = base[zz, g * group + n, c] + w1 * ss[n]
+                        y2 = y * y
+                        t = jnp.tanh(y * (KY + y2))
                         up = 1.0 + t
-                        slope = up * (1.0 + x * (1.0 - t) * (K1 + 3.0 * K3 * x2))
-                        sums[0][n] = sums[0][n] + half * (x * up)
+                        slope = up * (1.0 / 3.0 + (1.0 - t) * (y * (KY / 3.0 + y2)))
+                        sums[0][n] = sums[0][n] + half * (y * up)
                         sums[1][n] = sums[1][n] + h0 * slope
                         sums[2][n] = sums[2][n] + h1 * slope
                         sums[3][n] = sums[3][n] + h2 * slope
                 return tuple(tuple(s) for s in sums)
 
-            zero = tuple(jnp.zeros((own, LANES), F32) for _ in range(group))
+            zero = tuple(jnp.zeros((2 * own, LANES), F32) for _ in range(group))
             sums = lax.fori_loop(0, chans // unroll, channels, (zero,) * 4)
             for n, col in enumerate(cols):
-                fresh[:, col] = ds[n] + sums[0][n]
-                for k in range(3):
-                    slopes[k, z, :, col] = sums[k + 1][n]
+                for m in range(2):
+                    half_rows = slice(m * own, (m + 1) * own)
+                    fresh[half_rows, col] = dual[2 * zz + m, :, col] + sums[0][n][half_rows]
+                    for k in range(3):
+                        slopes[k, 2 * zz + m, :, col] = sums[k + 1][n][half_rows]
             return carry
 
         lax.fori_loop(0, nb // group, dual_piece, 0)
-        take([fresh[:, b * LANES : (b + 1) * LANES] for b in range(nb)], z, homes)
+        for n in range(2):
+            half_rows = slice(n * own, (n + 1) * own)
+            take([fresh[half_rows, b * LANES : (b + 1) * LANES] for b in range(nb)], 2 * zz + n)
         return carry
 
-    lax.fori_loop(0, rows, dual_row, 0)
+    lax.fori_loop(0, rows // 2, dual_row, 0)
     send_windows(0)
 
     to_dense(back(0), hsend, 0)
@@ -295,8 +354,6 @@
         @pl.when(has)
         def _():
             side = 1 if step < 0 else 0
-            for copy in edge_copies(-step):
-                copy.wait_recv()
             total = jnp.zeros((edge, LANES), F32)
             for core in range(cores):
                 pltpu.make_async_remote_copy(
@@ -322,25 +379,17 @@
     keep_high = (gz < groups - 1).astype(F32)
 
     def pixel_piece(h, carry):
-        def at(ref, z):
-            return ref[pl.ds(pl.multiple_of((z + 2) * np_ + h * 8, 8), 8), :]
-
         def channel(c, sums):
             sums = [list(s) for s in sums]
             kin = [[kernel_in[k, i, c] for i in range(2)] for k in range(3)]
-            kout = [0.5 * kernel_out[k, c] for k in range(3)]
-            bias = kernel_bias[c]
             for z in range(-1, rows + 1):
-                x = bias + jnp.zeros((8, LANES), F32)
-                hid = None
+                y = pixel_base[h, c, z + 1]
                 for k in range(3):
-                    x = x + kin[k][0] * at(dense_primal, z + k - 1)
-                    x = x + kin[k][1] * at(dense_back, z + k - 1)
-                    term = kout[k] * at(dense_cot, z - k + 1)
-                    hid = term if hid is None else hid + term
-                x2 = x * x
-                t = jnp.tanh(x * (K1 + K3 * x2))
-                grad = hid * ((1.0 + t) * (1.0 + x * (1.0 - t) * (K1 + 3.0 * K3 * x2)))
+                    y = y + (SCALE * kin[k][1]) * dense_at(dense_back, z + k - 1, h)
+                y2 = y * y
+                t = jnp.tanh(y * (KY + y2))
+                slope = (1.0 + t) * (1.0 / 3.0 + (1.0 - t) * (y * (KY / 3.0 + y2)))
+                grad = pixel_hid[h, c, z + 1] * slope
                 if z < 0:
                     grad = grad * keep_low
                 if z == rows:
@@ -364,16 +413,17 @@
 
     project(image.astype(BF16), 1)
 
+    projected(1)
+
     def grad_row(z, carry):
-        homes = home_blocks()
         outs = []
-        for b, value in enumerate(place(1, z, homes)):
+        for b, value in enumerate(place(z)):
             col = slice(b * LANES, (b + 1) * LANES)
             value = value + cot_dual[z, :, col]
             grad_dual[z, :, col] = value + value * slopes[0, z, :, col]
             grad_data[z, :, col] = value * slopes[2, z, :, col]
             outs.append(value * slopes[1, z, :, col])
-        take(outs, z, homes)
+        take(outs, z)
         return carry
 
     lax.fori_loop(0, rows, grad_row, 0)
@@ -429,18 +479,28 @@
         np_ = pixels // LANES
         dma = pltpu.SemaphoreType.DMA
         vmem = pl.BlockSpec(memory_space=pltpu.VMEM)
-        smem = pl.BlockSpec(memory_space=pltpu.SMEM)
         window = (own * rows, LANES)
-        scratch = [
+        args = (primal, dual, data) + rest
+        smalls = [
+            pltpu.SMEM(x.shape, x.dtype) if 2 < n < 11 else pltpu.VMEM(x.shape, x.dtype)
+            for n, x in enumerate(args)
+        ]
+        chans = rest[3].shape[0]
+        scratch = smalls + [
+            dma((len(args),)),
+            pltpu.VMEM((rows // 2, bins // LANES, chans, 2 * own, LANES), F32),
+            pltpu.VMEM((np_ // 8, chans, rows + 2, 8, LANES), F32),
+            pltpu.VMEM((np_ // 8, chans, rows + 2, 8, LANES), F32),
+            pltpu.VMEM((tiles,) + window, F32),
             pltpu.VMEM(blocks.shape[1:], BF16),
-            pltpu.VMEM((2, tiles) + window, F32),
-            pltpu.VMEM((2, tiles) + window, F32),
+            pltpu.VMEM((2, tiles) + window, BF16),
+            pltpu.VMEM((2, tiles) + window, BF16),
             pltpu.VMEM((tiles,) + window, F32),
             pltpu.VMEM((2, tiles) + window, BF16),
             pltpu.VMEM((2, tiles) + window, BF16),
             pltpu.VMEM((3, rows, own, bins), F32),
-            pltpu.VMEM((own, bins), F32),
-            pltpu.VMEM((own, bins), F32),
+            pltpu.VMEM((2 * own, bins), F32),
+            pltpu.VMEM((2 * own, bins), F32),
             pltpu.VMEM((np_ * rows, LANES), F32),
             pltpu.VMEM((np_ * rows, LANES), F32),
             pltpu.VMEM(((rows + 4) * np_, LANES), F32),
@@ -465,11 +525,11 @@
                 shape((rows, own, bins), F32),
                 shape((rows, own, bins), F32),
             ),
-            in_specs=[vmem, vmem, vmem, pl.BlockSpec(memory_space=pl.ANY)] + [smem] * 8 + [vmem] * 2,
+            in_specs=[pl.BlockSpec(memory_space=pl.ANY)] * 14,
             out_specs=(vmem, vmem, vmem),
             scratch_shapes=scratch,
             compiler_params=pltpu.CompilerParams(
-                collective_id=0, has_side_effects=True, vmem_limit_bytes=48 * 2**20
+                collective_id=0, has_side_effects=True, vmem_limit_bytes=60 * 2**20
             ),
         )(primal, dual, data, blocks[0], *rest)
 

time: 78.1 us -> 70.8 us (0.907)
  local copies, waits for them, and re-layouts: 12.4 us -> 5.22 us
    unnamed x29 -> x3, local copies, waits for them, and re-layouts: 12.4 us -> 5.22 us
where the time goes in v1:
time: 70.8 us; the launch traced here: 70.5 us
  Pallas kernels  64.6 us (91%)
  local copies, waits for them, and re-layouts  5.22 us (7%)
    pallas_call x1, Pallas kernels, local(): pl.pallas_call(functools.partial(kernel, tiles, groups, cores), out_shape...  64.6 us
    unnamed x3, local copies, waits for them, and re-layouts  5.22 us

profile of v1, /device:TPU:0, one launch (start us, length us, event | category | flops | bytes accessed | tf_op | source)
XLA Modules:
  0.0 70.5 jit_solution(915234128636934289)
XLA Ops:
  0.6 64.6 %shard_map.157 = (f32[8,2048]{1,0:T(8,128)}, f32[8,8,2048]{2,1,0:T(8,128)}, f32[8,8,2048]{2,1,0:T(8,128)}) custom-call(f32[8,2048]{1,0:T(8,128)} %primal_hbm.1, f32[8,8,2048]{2,1,0:T(8,128)} %dual_hbm.1, f32[8,8,2048]{2,1,0:T(8,128)} %data_hbm.1, bf16[32,2048,128]{2,1,0:T(8,128)(2,1)} %bitcast.1, s32[4,32]{1,0:T(4,128)} %offsets_hbm.1, ...), custom_call_target="tpu_custom_call" | custom-call | tf_op jit(solution)/shard_map/pallas_call | solution.py:521
  65.3 1.5 %copy.20 = f32[8,2048]{1,0:T(8,128)} copy(f32[8,2048]{1,0:T(8,128)} %get-tuple-element.6) | data formatting | bytes 131072
  66.8 1.9 %copy.21 = f32[8,8,2048]{2,1,0:T(8,128)} copy(f32[8,8,2048]{2,1,0:T(8,128)} %get-tuple-element.7) | data formatting | bytes 1048576
  68.6 1.9 %copy.22 = f32[8,8,2048]{2,1,0:T(8,128)} copy(f32[8,8,2048]{2,1,0:T(8,128)} %get-tuple-element.8) | data formatting | bytes 1048576
